TPU v7x, 256 devices: a whole 4x4x8 slice. The times are simulated.
256 devices in a mesh: row: 16 (over y, x_hi, core), col: 16 (over x_lo, z).
Axes of the slice: x: 4 (x_hi: 2, x_lo: 2; x = x_hi * 2 + x_lo), y: 4, z: 8, core: 2. Of those that a mesh axis runs over, the one named last changes fastest.
Arguments:
- grad_out: bfloat16 [65536, 256], P(('row', 'col')), may hold values from -6 to 6
- pre_act: bfloat16 [65536, 256], P(('row', 'col')), may hold values from -6 to 6
- features: bfloat16 [16, 4096, 256], P('col', 'row'), may hold values from -6 to 6
- weight: bfloat16 [256, 256], replicated, may hold values from -0.375 to 0.375
- tiles: bfloat16 [16, 16, 256, 128, 128], P('row', 'col'), may hold values from -0.078125 to 0.078125
- live: int32 [16, 16], P('row', 'col'), may hold values from 64 to 256, as said below
- block_row: int32 [16, 16, 256], P('row', 'col'), may hold values from 0 to 31, as said below
- block_col: int32 [16, 16, 256], P('row', 'col'), may hold values from 0 to 31
Outputs:
- grad_features: bfloat16 [16, 4096, 256], P('col', 'row')
- grad_weight: float32 [256, 256], replicated
Inputs may be any that keep to these rules, and one draw needn't show every extreme that they name: `live`: one tile has exactly 256 nonzero blocks. Within one tile the 256 pairs (block_row, block_col) are all different.
All inputs are finite; a program needn't handle non-finite values.
Results may differ from a plain program's by a relative error of at most 0.02.
Values may be sent and summed in bfloat16 or wider, within the bound.
A program may use at most 128 MiB of HBM per device.

v0:
```python
import jax
import jax.numpy as jnp
from jax import lax
from jax.sharding import PartitionSpec as P

SHARE = 8


def shards(grad_out, pre_act, features, weight, tiles, live, block_row, block_col):
    saved_grad, saved_pre = (
        lax.all_gather(grad_out, "col", axis=0, tiled=True),
        lax.all_gather(pre_act, "col", axis=0, tiled=True),
    )
    grad_block = jnp.where(saved_pre > 0, saved_grad, jnp.zeros_like(saved_grad))
    block_size = tiles.shape[-1]
    width = grad_block.shape[1]
    panel = features.shape[1]
    row_blocks = grad_block.reshape(-1, block_size, width)
    col_blocks = panel * lax.axis_size("row") // block_size
    tile_set = tiles[0, 0]
    rows_idx = block_row[0, 0]
    cols_idx = block_col[0, 0]
    count = live[0, 0]
    group = rows_idx.shape[0] // SHARE

    def add_group(number, total):
        first = number * group
        tile_part = lax.dynamic_slice_in_dim(tile_set, first, group, 0)
        rows_part = lax.dynamic_slice_in_dim(rows_idx, first, group, 0)
        cols_part = lax.dynamic_slice_in_dim(cols_idx, first, group, 0)
        gathered = jnp.take(row_blocks, rows_part, axis=0)
        contrib = jnp.einsum(
            "guv,guf->gvf", tile_part, gathered, preferred_element_type=jnp.float32
        )
        keep = first + jnp.arange(group, dtype=jnp.int32) < count
        contrib = jnp.where(keep[:, None, None], contrib, 0.0)
        return total.at[cols_part].add(contrib)

    start_total = jnp.zeros((col_blocks, block_size, width), jnp.float32)
    rounds = SHARE
    summed = lax.fori_loop(0, rounds, add_group, start_total)
    flat_terms = summed.reshape(col_blocks * block_size, width)
    scale = float(panel * lax.axis_size("row") * lax.axis_size("col")) ** (-0.5)
    back = lax.psum_scatter(
        flat_terms.astype(jnp.bfloat16), "row", scatter_dimension=0, tiled=True
    ).astype(jnp.float32)
    weight_term = jnp.dot(features[0].astype(jnp.float32).T, back, precision=lax.Precision.HIGHEST)
    grad_weight = lax.psum(weight_term, ("row", "col")) * scale
    grad_features = jnp.dot(
        back.astype(jnp.bfloat16), weight.T, preferred_element_type=jnp.float32
    ).astype(jnp.bfloat16)
    return (grad_features[None], grad_weight)


def solution(mesh):
    in_specs = (
        P(("row", "col"), None),
        P(("row", "col"), None),
        P("col", "row", None),
        P(),
        P("row", "col", None, None, None),
        P("row", "col"),
        P("row", "col", None),
        P("row", "col", None),
    )
    out_specs = (P("col", "row", None), P())
    return jax.shard_map(shards, mesh=mesh, in_specs=in_specs, out_specs=out_specs, check_vma=False)
```

profile of v0, /device:TPU:1, one launch (start us, length us, event | category | flops | bytes accessed | tf_op | source)
XLA Modules:
  0.0 640.8 jit_solution(17681159006061226467)
XLA Ops:
  7.2 0.0 copy-start
  7.2 0.0 all-gather.5.cloned.1.call-start
  7.2 0.7 all-gather.5.cloned.1.call-update
  7.9 0.0 all-gather.3.cloned.1.call-start
  8.0 0.7 all-gather.3.cloned.1.call-update
  8.7 0.0 reduce-scatter.2.cloned.1.call-start
  8.7 12.0 %copy.10 = bf16[1,1,256,128,128]{3,4,2,1,0:T(8,128)(2,1)} copy(bf16[1,1,256,128,128]{4,3,2,1,0:T(8,128)(2,1)} %param.14) | data formatting | bytes 16777216 | tf_op args[4]
  20.7 54.8 %all-gather.5.cloned.1.call-done = bf16[4096,256]{1,0:T(8,128)(2,1)} async-done(((bf16[256,256]{1,0:T(8,128)(2,1)}), bf16[4096,256]{1,0:T(8,128)(2,1)}) %all-gather.5.cloned.1.call-update) | async-done | bytes 2097168 | tf_op jit(solution)/shard_map/all_gather | solution.py:11
  75.5 70.6 %all-gather.3.cloned.1.call-done = bf16[4096,256]{1,0:T(8,128)(2,1)} async-done(((bf16[256,256]{1,0:T(8,128)(2,1)}), bf16[4096,256]{1,0:T(8,128)(2,1)}) %all-gather.3.cloned.1.call-update) | async-done | bytes 2097168 | tf_op jit(solution)/shard_map/all_gather | solution.py:12
  146.1 3.8 compare_select_fusion.2
  149.9 2.4 broadcast_in_dim.66
  152.3 136.0 %while.13 = (s32[]{:T(128)}, f32[32,128,256]{2,1,0:T(8,128)}, s32[256]{0:T(256)S(1)}, s32[]{:T(128)}, bf16[256,128,128]{1,2,0:T(8,128)(2,1)}, /*index=5*/s32[256...) while((s32[]{:T(128)}, f32[32,128,256]{2,1,0:T(8,128)}, ...), condition=%wide.region_2.3_spmd, body=%wide.region_0.2_spmd.sunk | while | flops 271582560 | bytes 24122544 | solution.py:41
  152.3 0.1 compare_select_fusion.5
  152.4 0.7 compare_and_fusion.2
  153.1 2.3 gather_fusion
  155.4 4.0 convolution_select_fusion.2
  159.4 9.8 %scatter_fusion = f32[32,128,256]{2,1,0:T(8,128)} fusion(f32[32,128,256]{2,1,0:T(8,128)} %get-tuple-element.207, s32[32]{0:T(128)S(1)} %compare_select_fusion.5, f32[32,128,256]{2,1,0:T(8,128)} %convolution_select_fusion.2), kind=kCustom, calls=%fused_computation.1.clone.1 | custom fusion | flops 1048576 | bytes 12583040 | tf_op jit(solution)/shard_map/while/body/eval_jaxpr/scatter-add | solution.py:37
  169.1 0.1 compare_select_fusion.5
  169.2 0.7 compare_and_fusion.2
  170.0 2.3 gather_fusion
  172.2 4.0 convolution_select_fusion.2
  176.2 9.9 %scatter_fusion = f32[32,128,256]{2,1,0:T(8,128)} fusion(f32[32,128,256]{2,1,0:T(8,128)} %get-tuple-element.207, s32[32]{0:T(128)S(1)} %compare_select_fusion.5, f32[32,128,256]{2,1,0:T(8,128)} %convolution_select_fusion.2), kind=kCustom, calls=%fused_computation.1.clone.1 | custom fusion | flops 1048576 | bytes 12583040 | tf_op jit(solution)/shard_map/while/body/eval_jaxpr/scatter-add | solution.py:37
  186.1 0.1 compare_select_fusion.5
  186.2 0.7 compare_and_fusion.2
  186.9 2.3 gather_fusion
  189.2 4.0 convolution_select_fusion.2
  193.2 9.9 %scatter_fusion = f32[32,128,256]{2,1,0:T(8,128)} fusion(f32[32,128,256]{2,1,0:T(8,128)} %get-tuple-element.207, s32[32]{0:T(128)S(1)} %compare_select_fusion.5, f32[32,128,256]{2,1,0:T(8,128)} %convolution_select_fusion.2), kind=kCustom, calls=%fused_computation.1.clone.1 | custom fusion | flops 1048576 | bytes 12583040 | tf_op jit(solution)/shard_map/while/body/eval_jaxpr/scatter-add | solution.py:37
  203.1 0.1 compare_select_fusion.5
  203.2 0.7 compare_and_fusion.2
  203.9 2.3 gather_fusion
  206.2 4.0 convolution_select_fusion.2
  210.2 10.1 %scatter_fusion = f32[32,128,256]{2,1,0:T(8,128)} fusion(f32[32,128,256]{2,1,0:T(8,128)} %get-tuple-element.207, s32[32]{0:T(128)S(1)} %compare_select_fusion.5, f32[32,128,256]{2,1,0:T(8,128)} %convolution_select_fusion.2), kind=kCustom, calls=%fused_computation.1.clone.1 | custom fusion | flops 1048576 | bytes 12583040 | tf_op jit(solution)/shard_map/while/body/eval_jaxpr/scatter-add | solution.py:37
  220.3 0.1 compare_select_fusion.5
  220.3 0.7 compare_and_fusion.2
  221.1 2.3 gather_fusion
  223.3 4.0 convolution_select_fusion.2
  227.3 9.9 %scatter_fusion = f32[32,128,256]{2,1,0:T(8,128)} fusion(f32[32,128,256]{2,1,0:T(8,128)} %get-tuple-element.207, s32[32]{0:T(128)S(1)} %compare_select_fusion.5, f32[32,128,256]{2,1,0:T(8,128)} %convolution_select_fusion.2), kind=kCustom, calls=%fused_computation.1.clone.1 | custom fusion | flops 1048576 | bytes 12583040 | tf_op jit(solution)/shard_map/while/body/eval_jaxpr/scatter-add | solution.py:37
  237.2 0.1 compare_select_fusion.5
  237.3 0.7 compare_and_fusion.2
  238.1 2.3 gather_fusion
  240.3 4.0 convolution_select_fusion.2
  244.3 9.9 %scatter_fusion = f32[32,128,256]{2,1,0:T(8,128)} fusion(f32[32,128,256]{2,1,0:T(8,128)} %get-tuple-element.207, s32[32]{0:T(128)S(1)} %compare_select_fusion.5, f32[32,128,256]{2,1,0:T(8,128)} %convolution_select_fusion.2), kind=kCustom, calls=%fused_computation.1.clone.1 | custom fusion | flops 1048576 | bytes 12583040 | tf_op jit(solution)/shard_map/while/body/eval_jaxpr/scatter-add | solution.py:37
  254.2 0.1 compare_select_fusion.5
  254.3 0.7 compare_and_fusion.2
  255.0 2.3 gather_fusion
  257.3 4.0 convolution_select_fusion.2
  261.3 9.9 %scatter_fusion = f32[32,128,256]{2,1,0:T(8,128)} fusion(f32[32,128,256]{2,1,0:T(8,128)} %get-tuple-element.207, s32[32]{0:T(128)S(1)} %compare_select_fusion.5, f32[32,128,256]{2,1,0:T(8,128)} %convolution_select_fusion.2), kind=kCustom, calls=%fused_computation.1.clone.1 | custom fusion | flops 1048576 | bytes 12583040 | tf_op jit(solution)/shard_map/while/body/eval_jaxpr/scatter-add | solution.py:37
  271.2 0.1 compare_select_fusion.5
  271.3 0.7 compare_and_fusion.2
  272.0 2.3 gather_fusion
  274.3 4.0 convolution_select_fusion.2
  278.3 9.9 %scatter_fusion = f32[32,128,256]{2,1,0:T(8,128)} fusion(f32[32,128,256]{2,1,0:T(8,128)} %get-tuple-element.207, s32[32]{0:T(128)S(1)} %compare_select_fusion.5, f32[32,128,256]{2,1,0:T(8,128)} %convolution_select_fusion.2), kind=kCustom, calls=%fused_computation.1.clone.1 | custom fusion | flops 1048576 | bytes 12583040 | tf_op jit(solution)/shard_map/while/body/eval_jaxpr/scatter-add | solution.py:37
  288.3 3.9 convert_element_type.12
  292.1 0.0 reduce-scatter.2.cloned.1.call-update
  292.1 0.0 all-reduce.2.cloned.1.call-start
  292.2 83.5 %reduce-scatter.2.cloned.1.call-done = bf16[256,256]{1,0:T(8,128)(2,1)} async-done(((bf16[4096,256]{1,0:T(8,128)(2,1)}), bf16[256,256]{1,0:T(8,128)(2,1)}) %reduce-scatter.2.cloned.1.call-update) | async-done | bytes 131088 | tf_op jit(solution)/shard_map/reduce_scatter | solution.py:44
  375.7 0.0 copy-done
  375.7 1.8 convolution_bitcast_fusion
  377.5 0.0 all-reduce.2.cloned.1.call-update
  377.6 0.0 copy-done.1
  377.6 1.8 fusion.6
  379.3 253.1 %all-reduce.2.cloned.1.call-done = f32[256,256]{0,1:T(8,128)} async-done(((f32[256,256]{0,1:T(8,128)}), f32[256,256]{0,1:T(8,128)}) %all-reduce.2.cloned.1.call-update) | async-done | bytes 262160 | tf_op jit(solution)/shard_map/psum | solution.py:48
  632.4 1.0 broadcast_multiply_fusion
  633.4 0.8 copy.11
  (13 shorter events, 0.1 us)
Async XLA Ops:
  7.2 368.5 %copy-start = (bf16[1,256,256]{2,1,0:T(8,128)(2,1)S(1)}, bf16[1,256,256]{2,1,0:T(8,128)(2,1)}, u32[]{:S(2)}) copy-start(bf16[1,256,256]{2,1,0:T(8,128)(2,1)} %param.12) | copy-start | bytes 393220
  7.2 68.3 %all-gather.5.cloned.1.call-start = ((), (), s32[]{:S(2)}) async-start(), calls=%async_computation.2 | async-start | bytes 2228224 | tf_op jit(solution)/shard_map/all_gather | solution.py:11
  7.9 138.2 %all-gather.3.cloned.1.call-start = ((), (), s32[]{:S(2)}) async-start(), calls=%async_computation.1 | async-start | bytes 2228224 | tf_op jit(solution)/shard_map/all_gather | solution.py:12
  8.7 367.0 %reduce-scatter.2.cloned.1.call-start = ((), (), s32[]{:S(2)}) async-start(), calls=%async_computation.3 | async-start | bytes 2228224 | tf_op jit(solution)/shard_map/reduce_scatter | solution.py:44
  20.7 131.6 %copy-start.2 = (s32[1,1,256]{2,1,0:T(1,128)S(1)}, s32[1,1,256]{2,1,0:T(1,128)}, u32[]{:S(2)}) copy-start(s32[1,1,256]{2,1,0:T(1,128)} %param.16) | copy-start | bytes 3076
  20.7 131.6 %copy-start.3 = (s32[1,1,256]{2,1,0:T(1,128)S(1)}, s32[1,1,256]{2,1,0:T(1,128)}, u32[]{:S(2)}) copy-start(s32[1,1,256]{2,1,0:T(1,128)} %param.17) | copy-start | bytes 3076
  288.3 89.3 %copy-start.1 = (bf16[256,256]{1,0:T(8,128)(2,1)S(1)}, bf16[256,256]{1,0:T(8,128)(2,1)}, u32[]{:S(2)}) copy-start(bf16[256,256]{1,0:T(8,128)(2,1)} %param.13) | copy-start | bytes 393220
  292.1 340.3 %all-reduce.2.cloned.1.call-start = ((), (), s32[]{:S(2)}) async-start(), calls=%async_computation.4 | async-start | bytes 524288 | tf_op jit(solution)/shard_map/psum | solution.py:48
Sparse Core Ops, SparseCore 0:
  9.8 65.6 all-gather.4
  77.3 68.7 all-gather.2
  292.3 83.3 reduce-scatter.1
  382.5 249.8 all-reduce.1
where the time goes:
time: 643 us; the launch traced here: 641 us
  waiting for transfers between devices  463 us (72%)
  other arithmetic  94.5 us (15%)
  matrix products  35.5 us (6%)
  local copies, waits for them, and re-layouts  33.4 us (5%)
  between operations  13.8 us (2%)
    psum x1, waiting for transfers between devices, shards(): grad_weight = lax.psum(weight_term, ('row', 'col')) * scale  253 us
    reduce_scatter x1, waiting for transfers between devices, shards(): lax.psum_scatter(flat_terms.astype(jnp.bfloat16), 'row', scatter_dimensio...  83.5 us
    scatter-add x8, other arithmetic, add_group(): return total.at[cols_part].add(contrib)  79.4 us
    all_gather x1, waiting for transfers between devices, shards(): lax.all_gather(pre_act, 'col', axis=0, tiled=True)  70.6 us
    all_gather x1, waiting for transfers between devices, shards(): lax.all_gather(grad_out, 'col', axis=0, tiled=True)  54.8 us
    dot_general x8, matrix products, add_group(): jnp.einsum('guv,guf->gvf', tile_part, gathered, preferred_element_type=jn...  31.8 us
    gather x8, local copies, waits for them, and re-layouts, add_group(): gathered = jnp.take(row_blocks, rows_part, axis=0)  18.2 us
  transfers between devices with their start and end apart: 4, of which 4 were waited for; matrix products, arithmetic and copies ran while one was open for 2% of the time, Pallas kernels for 0%

commit v1 on v0

v1 whole, which is shorter than its diff:
```python
import functools

import jax
import jax.numpy as jnp
from jax import lax
from jax.experimental import pallas as pl
from jax.experimental.pallas import tpu as pltpu
from jax.sharding import PartitionSpec as P

MESH = pl.DeviceIdType.MESH
F32 = jnp.float32
BF16 = jnp.bfloat16

F = 256
B = 128
NB = 32
LISTED = 256
NR = 16
NC = 16
STEPS = 4

N_AG = 34


def kernel(go_ref, pre_ref, feat_ref, w_ref, tiles_ref, live_ref, brow_ref, bcol_ref,
           gf_ref, gw_ref,
           tiles_v, gt, acc, idx_v, idx_s, featt, wt,
           sb1, rb1, ysend, yrecv, xsend, xrecv,
           gsum, grow, grow_in, gcol, gcol_in, gall,
           tile_sem, idx_sem, ag_send, ag_recv, s1_send, s1_recv, y_send, y_recv, x_send, x_recv,
           r_send, r_recv, c_send, c_recv, b_send, b_recv):
    i = lax.axis_index("row")
    j = lax.axis_index("col")
    y, xh, c = i // 4, (i // 2) % 2, i % 2
    xl, z = j // 8, j % 8

    def row_of(yy, xx, cc):
        return (yy * 2 + xx) * 2 + cc

    z_up = (i, xl * 8 + (z + 1) % 8)
    z_dn = (i, xl * 8 + (z + 7) % 8)
    x_peer = (i, (1 - xl) * 8 + z)
    core_peer = (row_of(y, xh, 1 - c), j)
    y_up = (row_of((y + 1) % 4, xh, c), j)
    y_dn = (row_of((y + 3) % 4, xh, c), j)
    xh_peer = (row_of(y, 1 - xh, c), j)

    tile_copy = pltpu.make_async_copy(tiles_ref.at[0, 0], tiles_v.at[pl.ds(0, LISTED)], tile_sem)
    tile_copy.start()

    barrier = pltpu.get_barrier_semaphore()

    @pl.loop(1, 16)
    def _(d):
        pl.semaphore_signal(barrier, inc=1, device_id=((i + d) % NR, j), device_id_type=MESH)
        pl.semaphore_signal(barrier, inc=1, device_id=(i, (j + d) % NC), device_id_type=MESH)

    g = jnp.where(pre_ref[...] > 0, go_ref[...], jnp.zeros_like(go_ref[...]))
    gT = g.T
    gt[2 * j] = gT[:, :B]
    gt[2 * j + 1] = gT[:, B:]

    pl.semaphore_wait(barrier, 30)

    sends = []

    def blk(dz, cls):
        zz = (z + dz + 16) % 8
        side = xl if cls in "AB" else 1 - xl
        return 2 * (side * 8 + zz) + (1 if cls in "BQ" else 0)

    def send(block, half, target, k):
        if half is None:
            src = gt.at[block]
        else:
            src = gt.at[block, pl.ds(half * B, B)]
        d = pltpu.make_async_remote_copy(src_ref=src, dst_ref=src, send_sem=ag_send.at[k], recv_sem=ag_recv.at[k],
                                         device_id=target, device_id_type=MESH)
        d.start()
        sends.append(d)
        return d

    CLS = "BAP"
    handle = {}

    def push(cls, s, src_up, src_dn):
        ci = CLS.index(cls)
        half_u = 0 if s == STEPS else None
        half_d = 1 if s == STEPS else None
        handle[(cls, s, "u")] = send(blk(src_up, cls), half_u, z_up, ci * 4 + s - 1)
        handle[(cls, s, "d")] = send(blk(src_dn, cls), half_d, z_dn, 12 + ci * 4 + s - 1)

    xa = send(blk(0, "A"), None, x_peer, 24)
    push("B", 1, 0, 0)
    push("A", 1, 0, 0)
    xb = {0: [send(blk(0, "B"), None, x_peer, 25)]}

    key = brow_ref[0] * NB + bcol_ref[0]
    lane = lax.broadcasted_iota(jnp.int32, (1, LISTED), 1)
    key = jnp.where(lane < live_ref[0, 0], key, -1)
    for h in range(2):
        kt = jnp.broadcast_to(key[:, h * B:(h + 1) * B], (B, B)).T
        number = lax.broadcasted_iota(jnp.int32, (B, B), 0) + h * B
        cell = lax.broadcasted_iota(jnp.int32, (B, B), 1)
        for q in range(8):
            found = jnp.where(kt == cell + q * B, number, LISTED)
            best = jnp.min(found, axis=0, keepdims=True)
            if h == 0:
                idx_v[q:q + 1, :] = best
            else:
                idx_v[q:q + 1, :] = jnp.minimum(idx_v[q:q + 1, :], best)
    idx_copy = pltpu.make_async_copy(idx_v, idx_s, idx_sem)
    idx_copy.start()
    tiles_v[LISTED] = jnp.zeros((B, B), BF16)
    featt[...] = feat_ref[0].T
    wt[...] = w_ref[...].T

    def product(blocks, d):
        parts_l, parts_r = [], []
        for b in blocks:
            parts_l.append(gt[b])
            q, o = b // 4, (b % 4) * NB
            left = tiles_v[idx_s[q, o + 2 * d]]
            right = tiles_v[idx_s[q, o + 2 * d + 1]]
            parts_r.append(jnp.concatenate([left, right], axis=1))
        return jnp.dot(jnp.concatenate(parts_l, axis=1), jnp.concatenate(parts_r, axis=0), preferred_element_type=F32)

    def blocks_of(s):
        if s == 0 or s == STEPS:
            return [blk(s, k) for k in "ABPQ"]
        return [blk(t, k) for t in (s, -s) for k in "ABPQ"]

    def work(s, lo, hi):
        blocks = blocks_of(s)

        @pl.loop(lo, hi)
        def _(d):
            v = product(blocks, d)
            if s == 0:
                acc[d] = v
            else:
                acc[d] += v

    cuts = (0, 5, 10, 16)
    idx_copy.wait()
    tile_copy.wait()
    xa.wait_recv()
    push("P", 1, 0, 0)
    for s in range(1, STEPS + 1):
        for n, cls in enumerate(CLS):
            handle[(cls, s, "u")].wait_recv()
            handle[(cls, s, "d")].wait_recv()
            if s < STEPS:
                push(cls, s + 1, -s, s)
            if cls == "B":
                if s < STEPS:
                    xb[s] = [send(blk(-s, "B"), None, x_peer, 24 + 2 * s), send(blk(s, "B"), None, x_peer, 25 + 2 * s)]
                else:
                    xb[s] = [send(blk(s, "B"), 0, x_peer, 24 + 2 * s), send(blk(s, "B"), 1, x_peer, 25 + 2 * s)]
                for d in xb[s - 1]:
                    d.wait_recv()
            work(s - 1, cuts[n], cuts[n + 1])
    for d in xb[STEPS]:
        d.wait_recv()

    last = blocks_of(STEPS)
    DY = (2, 1, 3, 0)

    def core_copy(m):
        return pltpu.make_async_remote_copy(src_ref=sb1.at[m], dst_ref=rb1.at[m], send_sem=s1_send.at[m], recv_sem=s1_recv.at[m],
                                            device_id=core_peer, device_id_type=MESH)

    def dest(m, cc):
        p = m // 2
        dy = (2 + 3 * p + (p // 2) * 3 + (p // 3) * 2) % 4
        return row_of((y + dy) % 4, m % 2, cc)

    @pl.loop(0, 8)
    def _(m):
        d = dest(m, 1 - c)
        sb1[m] = (acc[d] + product(last, d)).astype(BF16)
        core_copy(m).start()

    @pl.loop(0, 8)
    def _(m):
        d = dest(m, c)
        acc[d] += product(last, d)

    def mine(m):
        return acc.at[dest(m, c)]

    ysends = []

    def y_copy(k, target):
        d = pltpu.make_async_remote_copy(src_ref=ysend.at[k], dst_ref=yrecv.at[k], send_sem=y_send.at[k], recv_sem=y_recv.at[k],
                                         device_id=target, device_id_type=MESH)
        d.start()
        ysends.append(d)
        return d

    h_a, h_b = pl.ds(0, B), pl.ds(B, B)
    yh = {}
    for m in range(8):
        core_copy(m).wait_recv()
        a = mine(m)
        p, xx = m // 2, m % 2
        if p == 0:
            v = (a[...] + rb1[m].astype(F32)).astype(BF16)
            ysend[0 + xx] = v[:B]
            yh[0 + xx] = y_copy(0 + xx, y_up)
            ysend[2 + xx] = v[B:]
            yh[2 + xx] = y_copy(2 + xx, y_dn)
        elif p == 1:
            v = a[...] + rb1[m].astype(F32)
            ysend[4 + xx] = v[B:].astype(BF16)
            yh[4 + xx] = y_copy(4 + xx, y_up)
            a[h_a, :] = v[:B]
        elif p == 2:
            v = a[...] + rb1[m].astype(F32)
            ysend[6 + xx] = v[:B].astype(BF16)
            yh[6 + xx] = y_copy(6 + xx, y_dn)
            a[h_b, :] = v[B:]
        else:
            a[...] += rb1[m].astype(F32)
    for xx in range(2):
        yh[0 + xx].wait_recv()
        ysend[8 + xx] = (mine(2 + xx)[h_a, :] + yrecv[0 + xx].astype(F32)).astype(BF16)
        yh[8 + xx] = y_copy(8 + xx, y_up)
        yh[2 + xx].wait_recv()
        ysend[10 + xx] = (mine(4 + xx)[h_b, :] + yrecv[2 + xx].astype(F32)).astype(BF16)
        yh[10 + xx] = y_copy(10 + xx, y_dn)
    for k in (4, 5, 6, 7, 8, 9, 10, 11):
        yh[k].wait_recv()

    def y_sum(xx, keep):
        top = acc[keep, h_a, :] + yrecv[6 + xx].astype(F32) + yrecv[8 + xx].astype(F32)
        bot = acc[keep, h_b, :] + yrecv[4 + xx].astype(F32) + yrecv[10 + xx].astype(F32)
        return top, bot

    def y_total(xx):
        keep = row_of(y, xx, c)
        top = acc[keep, h_a, :] + yrecv[6 + xx].astype(F32) + yrecv[8 + xx].astype(F32)
        bot = acc[keep, h_b, :] + yrecv[4 + xx].astype(F32) + yrecv[10 + xx].astype(F32)
        return top, bot

    top, bot = y_total(1 - xh)
    xsend[0:B] = top.astype(BF16)
    xsend[B:] = bot.astype(BF16)
    xc = pltpu.make_async_remote_copy(src_ref=xsend, dst_ref=xrecv, send_sem=x_send, recv_sem=x_recv,
                                      device_id=xh_peer, device_id_type=MESH)
    xc.start()
    top, bot = y_total(xh)
    xc.wait_recv()
    back = jnp.concatenate([top, bot], axis=0) + xrecv[...].astype(F32)
    back_t = back.astype(BF16).T
    gsum[...] = jnp.dot(featt[...], back_t, preferred_element_type=F32)
    gf_ref[0] = jnp.dot(back_t, wt[...], preferred_element_type=F32).astype(BF16)

    grow[...] = gsum[...].astype(BF16)

    def r_copy(d):
        to = (i + d) % NR
        return pltpu.make_async_remote_copy(src_ref=grow.at[pl.ds(pl.multiple_of(to * 16, 16), 16)], dst_ref=grow_in.at[d],
                                            send_sem=r_send.at[d], recv_sem=r_recv.at[d], device_id=(to, j), device_id_type=MESH)

    @pl.loop(1, NR)
    def _(d):
        r_copy(d).start()

    total = gsum[pl.ds(pl.multiple_of(i * 16, 16), 16), :]
    for d in range(1, NR):
        r_copy(d).wait_recv()
        total += grow_in[d].astype(F32)
    gcol[...] = total.astype(BF16)
    gcol_in[j] = total.astype(BF16)

    def c_copy(d):
        to = (j + d) % NC
        return pltpu.make_async_remote_copy(src_ref=gcol, dst_ref=gcol_in.at[j],
                                            send_sem=c_send.at[d], recv_sem=c_recv.at[d], device_id=(i, to), device_id_type=MESH)

    @pl.loop(1, NC)
    def _(d):
        c_copy(d).start()

    @pl.loop(1, NC)
    def _(d):
        c_copy(d).wait_recv()

    total = gcol_in[0].astype(F32)
    for d in range(1, NC):
        total += gcol_in[d].astype(F32)
    gall[i] = (total * (1.0 / 256.0)).astype(BF16)

    def b_copy(d):
        to = (i + d) % NR
        return pltpu.make_async_remote_copy(src_ref=gall.at[i], dst_ref=gall.at[i],
                                            send_sem=b_send.at[d], recv_sem=b_recv.at[d], device_id=(to, j), device_id_type=MESH)

    @pl.loop(1, NR)
    def _(d):
        b_copy(d).start()

    @pl.loop(1, NR)
    def _(d):
        b_copy(d).wait_recv()

    for d in range(NR):
        gw_ref[d * 16:(d + 1) * 16, :] = gall[d].astype(F32)

    for d in sends:
        d.wait_send()
    for d in ysends:
        d.wait_send()
    xc.wait_send()

    @pl.loop(0, 8)
    def _(m):
        core_copy(m).wait_send()

    @pl.loop(1, NR)
    def _(d):
        r_copy(d).wait_send()
        c_copy(d).wait_send()
        b_copy(d).wait_send()


def shards(grad_out, pre_act, features, weight, tiles, live, block_row, block_col):
    vmem = pl.BlockSpec(memory_space=pltpu.VMEM)
    return pl.pallas_call(
        kernel,
        out_shape=(jax.ShapeDtypeStruct((1, 256, F), BF16), jax.ShapeDtypeStruct((F, F), F32)),
        in_specs=[vmem, vmem, vmem, vmem, pl.BlockSpec(memory_space=pl.ANY), pl.BlockSpec(memory_space=pltpu.SMEM), vmem, vmem],
        out_specs=(vmem, vmem),
        scratch_shapes=[
            pltpu.VMEM((LISTED + 1, B, B), BF16),
            pltpu.VMEM((NB, F, B), BF16),
            pltpu.VMEM((NR, F, F), F32),
            pltpu.VMEM((8, B), jnp.int32),
            pltpu.SMEM((8, B), jnp.int32),
            pltpu.VMEM((F, F), BF16),
            pltpu.VMEM((F, F), BF16),
            pltpu.VMEM((8, F, F), BF16),
            pltpu.VMEM((8, F, F), BF16),
            pltpu.VMEM((12, B, F), BF16),
            pltpu.VMEM((12, B, F), BF16),
            pltpu.VMEM((F, F), BF16),
            pltpu.VMEM((F, F), BF16),
            pltpu.VMEM((F, F), F32),
            pltpu.VMEM((F, F), BF16),
            pltpu.VMEM((NR, 16, F), BF16),
            pltpu.VMEM((16, F), BF16),
            pltpu.VMEM((NC, 16, F), BF16),
            pltpu.VMEM((NR, 16, F), BF16),
            pltpu.SemaphoreType.DMA,
            pltpu.SemaphoreType.DMA,
            pltpu.SemaphoreType.DMA((N_AG,)),
            pltpu.SemaphoreType.DMA((N_AG,)),
            pltpu.SemaphoreType.DMA((8,)),
            pltpu.SemaphoreType.DMA((8,)),
            pltpu.SemaphoreType.DMA((12,)),
            pltpu.SemaphoreType.DMA((12,)),
            pltpu.SemaphoreType.DMA,
            pltpu.SemaphoreType.DMA,
            pltpu.SemaphoreType.DMA((NR,)),
            pltpu.SemaphoreType.DMA((NR,)),
            pltpu.SemaphoreType.DMA((NC,)),
            pltpu.SemaphoreType.DMA((NC,)),
            pltpu.SemaphoreType.DMA((NR,)),
            pltpu.SemaphoreType.DMA((NR,)),
        ],
        compiler_params=pltpu.CompilerParams(collective_id=0, has_side_effects=True, vmem_limit_bytes=48 * 1024 * 1024),
        cost_estimate=pl.CostEstimate(flops=2 * 4096 * 4096 * 256, bytes_accessed=10 * 1024 * 1024, transcendentals=0),
    )(grad_out, pre_act, features, weight, tiles, live, block_row, block_col)


def solution(mesh):
    in_specs = (
        P(("row", "col"), None),
        P(("row", "col"), None),
        P("col", "row", None),
        P(),
        P("row", "col", None, None, None),
        P("row", "col"),
        P("row", "col", None),
        P("row", "col", None),
    )
    out_specs = (P("col", "row", None), P())
    return jax.shard_map(shards, mesh=mesh, in_specs=in_specs, out_specs=out_specs, check_vma=False)
```

time: 643 us -> 81.9 us (0.13)
  waiting for transfers between devices: 463 us -> 0 us
  other arithmetic: 94.5 us -> 0 us
  Pallas kernels: 0 us -> 74.1 us
  matrix products: 35.5 us -> 0 us
  local copies, waits for them, and re-layouts: 33.4 us -> 6.33 us
  between operations: 13.8 us -> 1.3 us
    psum x1 -> x0, waiting for transfers between devices: 253 us -> none  [shards(): grad_weight = lax.psum(weight_term, ('row', 'col')) * scale]
    all_gather x2 -> x0, waiting for transfers between devices: 125 us -> none  [the longest x1 70.6 us: shards(): lax.all_gather(pre_act, 'col', axis=0, tiled=True)]
    reduce_scatter x1 -> x0, waiting for transfers between devices: 83.5 us -> none  [shards(): lax.psum_scatter(flat_terms.astype(jnp.bfloat16), 'row', scatter_dimensio...]
    scatter-add x8 -> x0, other arithmetic: 79.4 us -> none  [add_group(): return total.at[cols_part].add(contrib)]
    pallas_call x0 -> x1, Pallas kernels: none -> 74.1 us  [shards(): pl.pallas_call(kernel, out_shape=(jax.ShapeDtypeStruct((1, 256, F), BF16)...]
    dot_general x10 -> x0, matrix products: 35.5 us -> none  [the longest x8 31.8 us: add_group(): jnp.einsum('guv,guf->gvf', tile_part, gathered, preferred_element_type=jn...]
    gather x8 -> x0, local copies, waits for them, and re-layouts: 18.2 us -> none  [add_group(): gathered = jnp.take(row_blocks, rows_part, axis=0)]
    unnamed x10 -> x14, local copies, waits for them, and re-layouts: 12.8 us -> 6.33 us
  transfers between devices with their start and end apart: 4 -> 0, of which waited for: 4 -> 0; matrix products, arithmetic and copies ran while one was open for 2% -> 0% of each run, Pallas kernels for 0% -> 0%
where the time goes in v1:
time: 81.9 us; the launch traced here: 81.7 us
  Pallas kernels  74.1 us (90%)
  local copies, waits for them, and re-layouts  6.33 us (8%)
  between operations  1.3 us (2%)
    pallas_call x1, Pallas kernels, shards(): pl.pallas_call(kernel, out_shape=(jax.ShapeDtypeStruct((1, 256, F), BF16)...  74.1 us
    unnamed x14, local copies, waits for them, and re-layouts  6.33 us

profile of v1, /device:TPU:1, one launch (start us, length us, event | category | flops | bytes accessed | tf_op | source)
XLA Modules:
  0.0 81.7 jit_solution(383578613988197975)
XLA Ops:
  1.3 0.0 copy-start
  1.3 0.9 %copy-done = bf16[256,256]{1,0:T(8,128)(2,1)S(1)} copy-done((bf16[256,256]{1,0:T(8,128)(2,1)S(1)}, bf16[256,256]{1,0:T(8,128)(2,1)}, u32[]{:S(2)}) %copy-start) | copy-done | bytes 131096
  2.2 0.0 copy-start.1
  2.2 0.9 %copy-done.1 = bf16[256,256]{1,0:T(8,128)(2,1)S(1)} copy-done((bf16[256,256]{1,0:T(8,128)(2,1)S(1)}, bf16[256,256]{1,0:T(8,128)(2,1)}, u32[]{:S(2)}) %copy-start.1) | copy-done | bytes 131096
  3.1 0.0 copy-start.2
  3.1 0.9 %copy-done.2 = bf16[1,256,256]{2,1,0:T(8,128)(2,1)S(1)} copy-done((bf16[1,256,256]{2,1,0:T(8,128)(2,1)S(1)}, bf16[1,256,256]{2,1,0:T(8,128)(2,1)}, u32[]{:S(2)}) %copy-start.2) | copy-done | bytes 131096
  4.0 0.0 copy-start.3
  4.0 0.9 %copy-done.3 = bf16[256,256]{1,0:T(8,128)(2,1)S(1)} copy-done((bf16[256,256]{1,0:T(8,128)(2,1)S(1)}, bf16[256,256]{1,0:T(8,128)(2,1)}, u32[]{:S(2)}) %copy-start.3) | copy-done | bytes 131096
  4.9 0.0 copy-start.4
  4.9 0.7 copy-done.4
  5.6 0.0 copy-start.5
  5.6 0.7 copy-done.5
  6.3 74.1 %shard_map.95 = (bf16[1,256,256]{2,1,0:T(8,128)(2,1)S(1)}, f32[256,256]{1,0:T(8,128)S(1)}) custom-call(bf16[256,256]{1,0:T(8,128)(2,1)S(1)} %copy-done, bf16[256,256]{1,0:T(8,128)(2,1)S(1)} %copy-done.1, bf16[1,256,256]{2,1,0:T(8,128)(2,1)S(1)} %copy-done.2, bf16[256,256]{1,0:T(8,128)(2,1)S(1)} %copy-done.3, bf16[1,1,256,128,128]{4,3,2,1,0:T(8,128)(2,1)} %tiles_ref.1, ...), custom_call_target="tpu_custom_call" | custom-call | flops 8589934592 | bytes 10485760 | tf_op jit(solution)/shard_map/pallas_call | solution.py:330
  80.3 0.7 copy.13
  81.0 0.7 copy.14
Async XLA Ops:
  1.3 0.9 %copy-start = (bf16[256,256]{1,0:T(8,128)(2,1)S(1)}, bf16[256,256]{1,0:T(8,128)(2,1)}, u32[]{:S(2)}) copy-start(bf16[256,256]{1,0:T(8,128)(2,1)} %go_ref.1) | copy-start | bytes 393220
  2.2 0.9 %copy-start.1 = (bf16[256,256]{1,0:T(8,128)(2,1)S(1)}, bf16[256,256]{1,0:T(8,128)(2,1)}, u32[]{:S(2)}) copy-start(bf16[256,256]{1,0:T(8,128)(2,1)} %pre_ref.1) | copy-start | bytes 393220
  3.1 0.9 %copy-start.2 = (bf16[1,256,256]{2,1,0:T(8,128)(2,1)S(1)}, bf16[1,256,256]{2,1,0:T(8,128)(2,1)}, u32[]{:S(2)}) copy-start(bf16[1,256,256]{2,1,0:T(8,128)(2,1)} %feat_ref.1) | copy-start | bytes 393220
  4.0 0.9 %copy-start.3 = (bf16[256,256]{1,0:T(8,128)(2,1)S(1)}, bf16[256,256]{1,0:T(8,128)(2,1)}, u32[]{:S(2)}) copy-start(bf16[256,256]{1,0:T(8,128)(2,1)} %w_ref.1) | copy-start | bytes 393220
  4.9 0.7 copy-start.4
  5.6 0.7 copy-start.5

commit v2 on v1

v2 whole, which is shorter than its diff:
```python
import functools

import jax
import jax.numpy as jnp
from jax import lax
from jax.experimental import pallas as pl
from jax.experimental.pallas import tpu as pltpu
from jax.sharding import PartitionSpec as P

MESH = pl.DeviceIdType.MESH
F32 = jnp.float32
BF16 = jnp.bfloat16

F = 256
B = 128
NB = 32
LISTED = 256
NR = 16
NC = 16
STEPS = 4

N_AG = 34


def kernel(go_hbm, pre_hbm, feat_hbm, w_hbm, tiles_ref, live_ref, brow_hbm, bcol_hbm,
           gf_ref, gw_ref,
           go_ref, pre_ref, w_ref, brow_ref, bcol_ref, in_sem,
           tiles_v, gt, acc, idx_v, idx_s, fv, wt,
           pb, rb1, yrecv,
           gsum, grow, grow_in, gcol_in, gall,
           tile_sem, idx_sem, ag_send, ag_recv, f_send, f_recv, s1_send, s1_recv, y_send, y_recv,
           r_send, r_recv, c_send, c_recv, b_send, b_recv):
    i = lax.axis_index("row")
    j = lax.axis_index("col")
    y, xh, c = i // 4, (i // 2) % 2, i % 2
    xl, z = j // 8, j % 8

    def row_of(yy, xx, cc):
        return (yy * 2 + xx) * 2 + cc

    z_up = (i, xl * 8 + (z + 1) % 8)
    z_dn = (i, xl * 8 + (z + 7) % 8)
    x_peer = (i, (1 - xl) * 8 + z)
    core_peer = (row_of(y, xh, 1 - c), j)
    y_up = (row_of((y + 1) % 4, xh, c), j)
    y_dn = (row_of((y + 3) % 4, xh, c), j)
    xh_peer = (row_of(y, 1 - xh, c), j)

    loads = [pltpu.make_async_copy(a, b, in_sem.at[k]) for k, (a, b) in enumerate((
        (go_hbm, go_ref), (pre_hbm, pre_ref), (brow_hbm, brow_ref), (bcol_hbm, bcol_ref), (feat_hbm.at[0], fv.at[i]), (w_hbm, w_ref)))]
    for load in loads:
        load.start()
    tile_copy = pltpu.make_async_copy(tiles_ref.at[0, 0], tiles_v.at[pl.ds(0, LISTED)], tile_sem)
    tile_copy.start()

    barrier = pltpu.get_barrier_semaphore()

    for near_by in (z_up, z_dn, x_peer, core_peer, y_up, y_dn, xh_peer):
        pl.semaphore_signal(barrier, inc=1, device_id=near_by, device_id_type=MESH)

    loads[0].wait()
    loads[1].wait()
    g = jnp.where(pre_ref[...] > 0, go_ref[...], jnp.zeros_like(go_ref[...]))
    gT = g.T
    gt[2 * j] = gT[:, :B]
    gt[2 * j + 1] = gT[:, B:]

    pl.semaphore_wait(barrier, 7)

    sends = []

    def blk(dz, cls):
        zz = (z + dz + 16) % 8
        side = xl if cls in "AB" else 1 - xl
        return 2 * (side * 8 + zz) + (1 if cls in "BQ" else 0)

    def send(block, half, target, k):
        if half is None:
            src = gt.at[block]
        else:
            src = gt.at[block, pl.ds(half * B, B)]
        d = pltpu.make_async_remote_copy(src_ref=src, dst_ref=src, send_sem=ag_send.at[k], recv_sem=ag_recv.at[k],
                                         device_id=target, device_id_type=MESH)
        d.start()
        sends.append(d)
        return d

    CLS = "BAP"
    handle = {}

    def push(cls, s, src_up, src_dn):
        ci = CLS.index(cls)
        half_u = 0 if s == STEPS else None
        half_d = 1 if s == STEPS else None
        handle[(cls, s, "u")] = send(blk(src_up, cls), half_u, z_up, ci * 4 + s - 1)
        handle[(cls, s, "d")] = send(blk(src_dn, cls), half_d, z_dn, 12 + ci * 4 + s - 1)

    xa = send(blk(0, "A"), None, x_peer, 24)
    push("B", 1, 0, 0)
    push("A", 1, 0, 0)
    xb = {0: [send(blk(0, "B"), None, x_peer, 25)]}

    for load in (loads[2], loads[3], loads[5]):
        load.wait()
    key = brow_ref[0] * NB + bcol_ref[0]
    lane = lax.broadcasted_iota(jnp.int32, (1, LISTED), 1)
    key = jnp.where(lane < live_ref[0, 0], key, -1)
    for h in range(2):
        kt = jnp.broadcast_to(key[:, h * B:(h + 1) * B], (B, B)).T
        number = lax.broadcasted_iota(jnp.int32, (B, B), 0) + h * B
        cell = lax.broadcasted_iota(jnp.int32, (B, B), 1)
        for q in range(8):
            found = jnp.where(kt == cell + q * B, number, LISTED)
            best = jnp.min(found, axis=0, keepdims=True)
            if h == 0:
                idx_v[q:q + 1, :] = best
            else:
                idx_v[q:q + 1, :] = jnp.minimum(idx_v[q:q + 1, :], best)
    idx_copy = pltpu.make_async_copy(idx_v, idx_s, idx_sem)
    idx_copy.start()
    tiles_v[LISTED] = jnp.zeros((B, B), BF16)
    wt[...] = w_ref[...].T

    def product(blocks, d):
        parts_l, parts_r = [], []
        for b in blocks:
            parts_l.append(gt[b])
            q, o = b // 4, (b % 4) * NB
            left = tiles_v[idx_s[q, o + 2 * d]]
            right = tiles_v[idx_s[q, o + 2 * d + 1]]
            parts_r.append(jnp.concatenate([left, right], axis=1))
        return jnp.dot(jnp.concatenate(parts_l, axis=1), jnp.concatenate(parts_r, axis=0), preferred_element_type=F32)

    def blocks_of(s):
        if s == 0 or s == STEPS:
            return [blk(s, k) for k in "ABPQ"]
        return [blk(t, k) for t in (s, -s) for k in "ABPQ"]

    def work(s, lo, hi, classes=None):
        blocks = blocks_of(s) if classes is None else [blk(s, k) for k in classes]

        @pl.loop(lo, hi, unroll=hi - lo)
        def _(d):
            v = product(blocks, d)
            if s == 0:
                acc[d] = v
            else:
                acc[d] += v

    fsends = []

    def fcopy(row, half, target, k):
        src = fv.at[row] if half is None else fv.at[row, pl.ds(half * B, B)]
        d = pltpu.make_async_remote_copy(src_ref=src, dst_ref=src, send_sem=f_send.at[k], recv_sem=f_recv.at[k],
                                         device_id=target, device_id_type=MESH)
        d.start()
        fsends.append(d)
        return d

    def near(dy, q):
        return row_of((y + dy + 4) % 4, (xh + q) % 2, c)

    def fpush(q, k):
        return fcopy(near(0, q), None, y_up, k), fcopy(near(0, q), None, y_dn, k + 1)

    def fcore(dy, q, k):
        return fcopy(near(dy, q), None, core_peer, k)

    loads[4].wait()
    f_x = fcopy(i, None, xh_peer, 0)
    f_own = fpush(0, 1)
    to_core = [fcore(0, 0, 9)]
    f_far = []

    def feature_step(n, f_x_):
        if n == 0:
            f_x_.wait_recv()
            pushed.append(fpush(1, 3))
            to_core.append(fcore(0, 1, 10))
        elif n == 1:
            for q in range(2):
                up, dn = (f_own, pushed[0])[q]
                up.wait_recv()
                f_far.append(fcopy(near(-1, q), 0, y_up, 5 + 2 * q))
                dn.wait_recv()
                f_far.append(fcopy(near(1, q), 1, y_dn, 6 + 2 * q))
                to_core.append(fcore(-1, q, 11 + 2 * q))
                to_core.append(fcore(1, q, 12 + 2 * q))
        else:
            for d in f_far:
                d.wait_recv()
            for q in range(2):
                to_core.append(fcore(2, q, 15 + q))

    pushed = []

    cuts = (0, 5, 10, 16)
    idx_copy.wait()
    tile_copy.wait()
    xa.wait_recv()
    push("P", 1, 0, 0)
    for s in range(1, STEPS + 1):
        for n, cls in enumerate(CLS):
            handle[(cls, s, "u")].wait_recv()
            handle[(cls, s, "d")].wait_recv()
            if s < STEPS:
                push(cls, s + 1, -s, s)
            if cls == "B":
                if s < STEPS:
                    xb[s] = [send(blk(-s, "B"), None, x_peer, 24 + 2 * s), send(blk(s, "B"), None, x_peer, 25 + 2 * s)]
                else:
                    xb[s] = [send(blk(s, "B"), 0, x_peer, 24 + 2 * s), send(blk(s, "B"), 1, x_peer, 25 + 2 * s)]
                for d in xb[s - 1]:
                    d.wait_recv()
            if cls == "A" and s > 1:
                feature_step(s - 2, f_x)
            work(s - 1, cuts[n], cuts[n + 1])
    for d in xb[STEPS]:
        d.wait_recv()

    last = blocks_of(STEPS)
    ORDER = ((2, 1), (2, 0), (1, 1), (3, 1), (0, 1), (1, 0), (3, 0), (0, 0))

    def core_copy(m):
        return pltpu.make_async_remote_copy(src_ref=pb.at[dest(m, 1 - c)], dst_ref=rb1.at[m], send_sem=s1_send.at[m], recv_sem=s1_recv.at[m],
                                            device_id=core_peer, device_id_type=MESH)

    def dest(m, cc):
        dy, q = ORDER[m]
        return row_of((y + dy) % 4, (xh + q) % 2, cc)

    for m in range(8):
        d = dest(m, 1 - c)
        pb[d] = (acc[d] + product(last, d)).astype(BF16)
        core_copy(m).start()
    for m in range(8):
        d = dest(m, c)
        pb[d] = (acc[d] + product(last, d)).astype(BF16)

    def each(copies, what):
        for copy in copies:
            getattr(copy, what)()

    for d in to_core:
        d.wait_recv()
    gt_sum = None
    for k in range(4):
        left = jnp.concatenate([pb[4 * k + n] for n in range(4)], axis=1)
        right = jnp.concatenate([fv[4 * k + n] for n in range(4)], axis=0)
        v = jnp.dot(left, right, preferred_element_type=F32)
        gt_sum = v if gt_sum is None else gt_sum + v
    gsum[...] = gt_sum.T
    grow[...] = gsum[...].astype(BF16)

    one, two = i, j

    def at(p, q):
        return (p, q)

    def r_copy(d):
        to = (one + d) % NR
        return pltpu.make_async_remote_copy(src_ref=grow.at[pl.ds(pl.multiple_of(to * 16, 16), 16)], dst_ref=grow_in.at[d],
                                            send_sem=r_send.at[d], recv_sem=r_recv.at[d], device_id=at(to, two), device_id_type=MESH)

    r_copies = [r_copy(d) for d in range(1, NR)]
    each(r_copies, "start")

    def y_copy(m):
        dy, q = ORDER[m]
        return pltpu.make_async_remote_copy(src_ref=pb.at[dest(m, c)], dst_ref=yrecv.at[m], send_sem=y_send.at[m], recv_sem=y_recv.at[m],
                                            device_id=(dest(m, c), j), device_id_type=MESH)

    core_copies = [core_copy(m) for m in range(8)]
    y_copies = [y_copy(m) for m in range(7)]
    for m in range(8):
        core_copies[m].wait_recv()
        d = dest(m, c)
        if m < 7:
            pb[d] = (pb[d].astype(F32) + rb1[m].astype(F32)).astype(BF16)
            y_copies[m].start()
        else:
            acc[d] = pb[d].astype(F32) + rb1[m].astype(F32)

    total = gsum[pl.ds(pl.multiple_of(one * 16, 16), 16), :]
    for n, copy in enumerate(r_copies):
        copy.wait_recv()
        total += grow_in[n + 1].astype(F32)
    gcol_in[two] = total.astype(BF16)

    def c_copy(d):
        to = (two + d) % NC
        return pltpu.make_async_remote_copy(src_ref=gcol_in.at[two], dst_ref=gcol_in.at[two],
                                            send_sem=c_send.at[d], recv_sem=c_recv.at[d], device_id=at(one, to), device_id_type=MESH)

    c_copies = [c_copy(d) for d in range(1, NC)]
    each(c_copies, "start")
    each(c_copies, "wait_recv")
    total = gcol_in[0].astype(F32)
    for d in range(1, NC):
        total += gcol_in[d].astype(F32)
    gall[one] = (total * (1.0 / 256.0)).astype(BF16)

    def b_copy(d):
        to = (one + d) % NR
        return pltpu.make_async_remote_copy(src_ref=gall.at[one], dst_ref=gall.at[one],
                                            send_sem=b_send.at[d], recv_sem=b_recv.at[d], device_id=at(to, two), device_id_type=MESH)

    b_copies = [b_copy(d) for d in range(1, NR)]
    each(b_copies, "start")

    each(y_copies, "wait_recv")
    back = acc[i]
    for m in range(7):
        back += yrecv[m].astype(F32)
    gf_ref[0] = jnp.dot(back.astype(BF16).T, wt[...], preferred_element_type=F32).astype(BF16)

    each(b_copies, "wait_recv")
    for d in range(NR):
        gw_ref[d * 16:(d + 1) * 16, :] = gall[d].astype(F32)

    each(sends + fsends + core_copies + y_copies + r_copies + c_copies + b_copies, "wait_send")


def shards(grad_out, pre_act, features, weight, tiles, live, block_row, block_col):
    vmem = pl.BlockSpec(memory_space=pltpu.VMEM)
    hbm = pl.BlockSpec(memory_space=pltpu.HBM)
    return pl.pallas_call(
        kernel,
        out_shape=(pltpu.VMEM((1, 256, F), BF16), pltpu.VMEM((F, F), F32)),
        in_specs=[hbm, hbm, hbm, hbm, hbm, pl.BlockSpec(memory_space=pltpu.SMEM), hbm, hbm],
        out_specs=(vmem, vmem),
        scratch_shapes=[
            pltpu.VMEM((256, F), BF16),
            pltpu.VMEM((256, F), BF16),
            pltpu.VMEM((F, F), BF16),
            pltpu.VMEM((1, 1, LISTED), jnp.int32),
            pltpu.VMEM((1, 1, LISTED), jnp.int32),
            pltpu.SemaphoreType.DMA((6,)),
            pltpu.VMEM((LISTED + 1, B, B), BF16),
            pltpu.VMEM((NB, F, B), BF16),
            pltpu.VMEM((NR, F, F), F32),
            pltpu.VMEM((8, B), jnp.int32),
            pltpu.SMEM((8, B), jnp.int32),
            pltpu.VMEM((NR, 256, F), BF16),
            pltpu.VMEM((F, F), BF16),
            pltpu.VMEM((NR, F, F), BF16),
            pltpu.VMEM((8, F, F), BF16),
            pltpu.VMEM((7, F, F), BF16),
            pltpu.VMEM((F, F), F32),
            pltpu.VMEM((F, F), BF16),
            pltpu.VMEM((NR, 16, F), BF16),
            pltpu.VMEM((NC, 16, F), BF16),
            pltpu.VMEM((NR, 16, F), BF16),
            pltpu.SemaphoreType.DMA,
            pltpu.SemaphoreType.DMA,
            pltpu.SemaphoreType.DMA((N_AG,)),
            pltpu.SemaphoreType.DMA((N_AG,)),
            pltpu.SemaphoreType.DMA((17,)),
            pltpu.SemaphoreType.DMA((17,)),
            pltpu.SemaphoreType.DMA((8,)),
            pltpu.SemaphoreType.DMA((8,)),
            pltpu.SemaphoreType.DMA((7,)),
            pltpu.SemaphoreType.DMA((7,)),
            pltpu.SemaphoreType.DMA((NR,)),
            pltpu.SemaphoreType.DMA((NR,)),
            pltpu.SemaphoreType.DMA((NC,)),
            pltpu.SemaphoreType.DMA((NC,)),
            pltpu.SemaphoreType.DMA((NR,)),
            pltpu.SemaphoreType.DMA((NR,)),
        ],
        compiler_params=pltpu.CompilerParams(collective_id=0, has_side_effects=True, vmem_limit_bytes=56 * 1024 * 1024),
        cost_estimate=pl.CostEstimate(flops=2 * 4096 * 4096 * 256, bytes_accessed=10 * 1024 * 1024, transcendentals=0),
    )(grad_out, pre_act, features, weight, tiles, live, block_row, block_col)


def solution(mesh):
    in_specs = (
        P(("row", "col"), None),
        P(("row", "col"), None),
        P("col", "row", None),
        P(),
        P("row", "col", None, None, None),
        P("row", "col"),
        P("row", "col", None),
        P("row", "col", None),
    )
    out_specs = (P("col", "row", None), P())
    return jax.shard_map(shards, mesh=mesh, in_specs=in_specs, out_specs=out_specs, check_vma=False)
```

time: 81.9 us -> 59.7 us (0.73)
  Pallas kernels: 74.1 us -> 57 us
  local copies, waits for them, and re-layouts: 6.33 us -> 1.36 us
    pallas_call x1, Pallas kernels: 74.1 us -> 57 us  [shards(): pl.pallas_call(kernel, out_shape=(pltpu.VMEM((1, 256, F), BF16), pltpu.VM...]
    unnamed x14 -> x2, local copies, waits for them, and re-layouts: 6.33 us -> 1.36 us
where the time goes in v2:
time: 59.7 us; the launch traced here: 59.6 us
  Pallas kernels  57 us (95%)
  local copies, waits for them, and re-layouts  1.36 us (2%)
  between operations  1.29 us (2%)
    pallas_call x1, Pallas kernels, shards(): pl.pallas_call(kernel, out_shape=(pltpu.VMEM((1, 256, F), BF16), pltpu.VM...  57 us
    unnamed x2, local copies, waits for them, and re-layouts  1.36 us

profile of v2, /device:TPU:1, one launch (start us, length us, event | category | flops | bytes accessed | tf_op | source)
XLA Modules:
  0.0 59.6 jit_solution(1600866737017645923)
XLA Ops:
  1.3 57.0 %shard_map.95 = (bf16[1,256,256]{2,1,0:T(8,128)(2,1)S(1)}, f32[256,256]{1,0:T(8,128)S(1)}) custom-call(bf16[256,256]{1,0:T(8,128)(2,1)} %go_hbm.1, bf16[256,256]{1,0:T(8,128)(2,1)} %pre_hbm.1, bf16[1,256,256]{2,1,0:T(8,128)(2,1)} %feat_hbm.1, bf16[256,256]{1,0:T(8,128)(2,1)} %w_hbm.1, bf16[1,1,256,128,128]{4,3,2,1,0:T(8,128)(2,1)} %tiles_ref.1, ...), custom_call_target="tpu_custom_call" | custom-call | flops 8589934592 | bytes 10485760 | tf_op jit(solution)/shard_map/pallas_call | solution.py:327
  58.2 0.7 %copy.12 = bf16[1,256,256]{2,1,0:T(8,128)(2,1)} copy(bf16[1,256,256]{2,1,0:T(8,128)(2,1)S(1)} %get-tuple-element.2) | data formatting | bytes 262144
  58.9 0.7 %copy.13 = f32[256,256]{1,0:T(8,128)} copy(f32[256,256]{1,0:T(8,128)S(1)} %get-tuple-element.3) | data formatting | bytes 524288

commit v3 on v2

--- a/solution.py
+++ b/solution.py
@@ -136,8 +136,8 @@
             return [blk(s, k) for k in "ABPQ"]
         return [blk(t, k) for t in (s, -s) for k in "ABPQ"]
 
-    def work(s, lo, hi, classes=None):
-        blocks = blocks_of(s) if classes is None else [blk(s, k) for k in classes]
+    def work(s, lo, hi, classes="ABPQ"):
+        blocks = [blk(t, k) for t in ((s, -s) if s else (0,)) for k in classes]
 
         @pl.loop(lo, hi, unroll=hi - lo)
         def _(d):
@@ -170,31 +170,36 @@
     f_x = fcopy(i, None, xh_peer, 0)
     f_own = fpush(0, 1)
     to_core = [fcore(0, 0, 9)]
-    f_far = []
-
-    def feature_step(n, f_x_):
-        if n == 0:
-            f_x_.wait_recv()
-            pushed.append(fpush(1, 3))
+    f_far = {}
+    f_xh = []
+
+    def f_around(q):
+        up, dn = (f_own, f_xh)[q]
+        up.wait_recv()
+        far_up = fcopy(near(-1, q), 0, y_up, 5 + 2 * q)
+        dn.wait_recv()
+        f_far[q] = (far_up, fcopy(near(1, q), 1, y_dn, 6 + 2 * q))
+        to_core.append(fcore(-1, q, 11 + 2 * q))
+        to_core.append(fcore(1, q, 12 + 2 * q))
+
+    def f_end(q):
+        for d in f_far[q]:
+            d.wait_recv()
+        to_core.append(fcore(2, q, 15 + q))
+
+    def feature_step(s, cls):
+        if (s, cls) == (1, "P"):
+            f_around(0)
+        elif (s, cls) == (2, "B"):
+            f_x.wait_recv()
+            f_xh.extend(fpush(1, 3))
             to_core.append(fcore(0, 1, 10))
-        elif n == 1:
-            for q in range(2):
-                up, dn = (f_own, pushed[0])[q]
-                up.wait_recv()
-                f_far.append(fcopy(near(-1, q), 0, y_up, 5 + 2 * q))
-                dn.wait_recv()
-                f_far.append(fcopy(near(1, q), 1, y_dn, 6 + 2 * q))
-                to_core.append(fcore(-1, q, 11 + 2 * q))
-                to_core.append(fcore(1, q, 12 + 2 * q))
-        else:
-            for d in f_far:
-                d.wait_recv()
-            for q in range(2):
-                to_core.append(fcore(2, q, 15 + q))
-
-    pushed = []
-
-    cuts = (0, 5, 10, 16)
+        elif (s, cls) == (3, "A"):
+            f_around(1)
+            f_end(0)
+        elif (s, cls) == (4, "P"):
+            f_end(1)
+
     idx_copy.wait()
     tile_copy.wait()
     xa.wait_recv()
@@ -212,9 +217,11 @@
                     xb[s] = [send(blk(s, "B"), 0, x_peer, 24 + 2 * s), send(blk(s, "B"), 1, x_peer, 25 + 2 * s)]
                 for d in xb[s - 1]:
                     d.wait_recv()
-            if cls == "A" and s > 1:
-                feature_step(s - 2, f_x)
-            work(s - 1, cuts[n], cuts[n + 1])
+            feature_step(s, cls)
+            if n < 2:
+                work(s - 1, 8 * n, 8 * n + 8, "PQ" if s > 1 else "ABPQ")
+            elif s < STEPS:
+                work(s, 0, NR, "AB")
     for d in xb[STEPS]:
         d.wait_recv()
 
@@ -241,28 +248,39 @@
         for copy in copies:
             getattr(copy, what)()
 
+    late = to_core.pop()
+    spots = [near(dy, q) for dy, q in ((0, 0), (0, 1), (1, 0), (3, 0), (1, 1), (3, 1), (2, 0), (2, 1))]
+    spots = [p + o for p in spots for o in (0, 1 - 2 * c)]
     for d in to_core:
         d.wait_recv()
     gt_sum = None
     for k in range(4):
-        left = jnp.concatenate([pb[4 * k + n] for n in range(4)], axis=1)
-        right = jnp.concatenate([fv[4 * k + n] for n in range(4)], axis=0)
+        if k == 3:
+            late.wait_recv()
+        left = jnp.concatenate([pb[p] for p in spots[4 * k:4 * k + 4]], axis=1)
+        right = jnp.concatenate([fv[p] for p in spots[4 * k:4 * k + 4]], axis=0)
         v = jnp.dot(left, right, preferred_element_type=F32)
         gt_sum = v if gt_sum is None else gt_sum + v
     gsum[...] = gt_sum.T
     grow[...] = gsum[...].astype(BF16)
 
-    one, two = i, j
-
-    def at(p, q):
-        return (p, q)
+    ROWS = [(dy, q, k) for dy, q in ((2, 1), (1, 1), (3, 1), (2, 0), (0, 1), (1, 0), (3, 0), (0, 0)) for k in (1, 0)][:15]
+    COLS = [(dz, k) for dz in (4, 3, 5, 2, 6, 1, 7, 0) for k in (1, 0)][:15]
+
+    def along_row(d):
+        dy, q, k = ROWS[d]
+        return row_of((y + dy) % 4, (xh + q) % 2, (c + k) % 2)
+
+    def along_col(d):
+        dz, k = COLS[d]
+        return ((xl + k) % 2) * 8 + (z + dz) % 8
 
     def r_copy(d):
-        to = (one + d) % NR
+        to = along_row(d)
         return pltpu.make_async_remote_copy(src_ref=grow.at[pl.ds(pl.multiple_of(to * 16, 16), 16)], dst_ref=grow_in.at[d],
-                                            send_sem=r_send.at[d], recv_sem=r_recv.at[d], device_id=at(to, two), device_id_type=MESH)
-
-    r_copies = [r_copy(d) for d in range(1, NR)]
+                                            send_sem=r_send.at[d], recv_sem=r_recv.at[d], device_id=(to, j), device_id_type=MESH)
+
+    r_copies = [r_copy(d) for d in range(15)]
     each(r_copies, "start")
 
     def y_copy(m):
@@ -272,40 +290,45 @@
 
     core_copies = [core_copy(m) for m in range(8)]
     y_copies = [y_copy(m) for m in range(7)]
-    for m in range(8):
-        core_copies[m].wait_recv()
-        d = dest(m, c)
-        if m < 7:
-            pb[d] = (pb[d].astype(F32) + rb1[m].astype(F32)).astype(BF16)
-            y_copies[m].start()
-        else:
-            acc[d] = pb[d].astype(F32) + rb1[m].astype(F32)
-
-    total = gsum[pl.ds(pl.multiple_of(one * 16, 16), 16), :]
+
+    def sums(lo, hi):
+        for m in range(lo, hi):
+            core_copies[m].wait_recv()
+            d = dest(m, c)
+            if m < 7:
+                pb[d] = (pb[d].astype(F32) + rb1[m].astype(F32)).astype(BF16)
+                y_copies[m].start()
+            else:
+                acc[d] = pb[d].astype(F32) + rb1[m].astype(F32)
+
+    sums(0, 4)
+
+    total = gsum[pl.ds(pl.multiple_of(i * 16, 16), 16), :]
     for n, copy in enumerate(r_copies):
         copy.wait_recv()
-        total += grow_in[n + 1].astype(F32)
-    gcol_in[two] = total.astype(BF16)
+        total += grow_in[n].astype(F32)
+    gcol_in[j] = total.astype(BF16)
 
     def c_copy(d):
-        to = (two + d) % NC
-        return pltpu.make_async_remote_copy(src_ref=gcol_in.at[two], dst_ref=gcol_in.at[two],
-                                            send_sem=c_send.at[d], recv_sem=c_recv.at[d], device_id=at(one, to), device_id_type=MESH)
-
-    c_copies = [c_copy(d) for d in range(1, NC)]
+        to = along_col(d)
+        return pltpu.make_async_remote_copy(src_ref=gcol_in.at[j], dst_ref=gcol_in.at[j],
+                                            send_sem=c_send.at[d], recv_sem=c_recv.at[d], device_id=(i, to), device_id_type=MESH)
+
+    c_copies = [c_copy(d) for d in range(15)]
     each(c_copies, "start")
+    sums(4, 8)
     each(c_copies, "wait_recv")
     total = gcol_in[0].astype(F32)
     for d in range(1, NC):
         total += gcol_in[d].astype(F32)
-    gall[one] = (total * (1.0 / 256.0)).astype(BF16)
+    gall[i] = (total * (1.0 / 256.0)).astype(BF16)
 
     def b_copy(d):
-        to = (one + d) % NR
-        return pltpu.make_async_remote_copy(src_ref=gall.at[one], dst_ref=gall.at[one],
-                                            send_sem=b_send.at[d], recv_sem=b_recv.at[d], device_id=at(to, two), device_id_type=MESH)
-
-    b_copies = [b_copy(d) for d in range(1, NR)]
+        to = along_row(d)
+        return pltpu.make_async_remote_copy(src_ref=gall.at[i], dst_ref=gall.at[i],
+                                            send_sem=b_send.at[d], recv_sem=b_recv.at[d], device_id=(to, j), device_id_type=MESH)
+
+    b_copies = [b_copy(d) for d in range(15)]
     each(b_copies, "start")
 
     each(y_copies, "wait_recv")

time: 59.7 us -> 58.8 us (0.985)
  Pallas kernels: 57 us -> 56.1 us
    pallas_call x1, Pallas kernels: 57 us -> 56.1 us  [shards(): pl.pallas_call(kernel, out_shape=(pltpu.VMEM((1, 256, F), BF16), pltpu.VM...]
where the time goes in v3:
time: 58.8 us; the launch traced here: 58.7 us
  Pallas kernels  56.1 us (95%)
  local copies, waits for them, and re-layouts  1.36 us (2%)
  between operations  1.29 us (2%)
    pallas_call x1, Pallas kernels, shards(): pl.pallas_call(kernel, out_shape=(pltpu.VMEM((1, 256, F), BF16), pltpu.VM...  56.1 us
    unnamed x2, local copies, waits for them, and re-layouts  1.36 us

profile of v3, /device:TPU:1, one launch (start us, length us, event | category | flops | bytes accessed | tf_op | source)
XLA Modules:
  0.0 58.7 jit_solution(2243623890971865384)
XLA Ops:
  1.3 56.1 %shard_map.95 = (bf16[1,256,256]{2,1,0:T(8,128)(2,1)S(1)}, f32[256,256]{1,0:T(8,128)S(1)}) custom-call(bf16[256,256]{1,0:T(8,128)(2,1)} %go_hbm.1, bf16[256,256]{1,0:T(8,128)(2,1)} %pre_hbm.1, bf16[1,256,256]{2,1,0:T(8,128)(2,1)} %feat_hbm.1, bf16[256,256]{1,0:T(8,128)(2,1)} %w_hbm.1, bf16[1,1,256,128,128]{4,3,2,1,0:T(8,128)(2,1)} %tiles_ref.1, ...), custom_call_target="tpu_custom_call" | custom-call | flops 8589934592 | bytes 10485760 | tf_op jit(solution)/shard_map/pallas_call | solution.py:350
  57.4 0.7 %copy.12 = bf16[1,256,256]{2,1,0:T(8,128)(2,1)} copy(bf16[1,256,256]{2,1,0:T(8,128)(2,1)S(1)} %get-tuple-element.2) | data formatting | bytes 262144
  58.0 0.7 %copy.13 = f32[256,256]{1,0:T(8,128)} copy(f32[256,256]{1,0:T(8,128)S(1)} %get-tuple-element.3) | data formatting | bytes 524288

commit v4 on v3

--- a/solution.py
+++ b/solution.py
@@ -264,21 +264,23 @@
     gsum[...] = gt_sum.T
     grow[...] = gsum[...].astype(BF16)
 
-    ROWS = [(dy, q, k) for dy, q in ((2, 1), (1, 1), (3, 1), (2, 0), (0, 1), (1, 0), (3, 0), (0, 0)) for k in (1, 0)][:15]
-    COLS = [(dz, k) for dz in (4, 3, 5, 2, 6, 1, 7, 0) for k in (1, 0)][:15]
-
-    def along_row(d):
-        dy, q, k = ROWS[d]
-        return row_of((y + dy) % 4, (xh + q) % 2, (c + k) % 2)
-
-    def along_col(d):
-        dz, k = COLS[d]
-        return ((xl + k) % 2) * 8 + (z + dz) % 8
+    ONES = [(dy, p, k) for dy, p in ((2, 1), (1, 1), (3, 1), (2, 0), (0, 1), (1, 0), (3, 0), (0, 0)) for k in (1, 0)][:15]
+    TWOS = [(4, 1), (3, 1), (5, 1), (4, 0), (2, 1), (6, 1), (1, 1), (7, 1), (3, 0), (5, 0), (0, 1), (2, 0), (6, 0), (1, 0), (7, 0)]
+    one, two = (y * 2 + xl) * 2 + c, xh * 8 + z
+
+    def along_one(d):
+        dy, p, k = ONES[d]
+        yy, pp, cc = (y + dy) % 4, (xl + p) % 2, (c + k) % 2
+        return (yy * 2 + pp) * 2 + cc, (row_of(yy, xh, cc), pp * 8 + z)
+
+    def along_two(d):
+        dz, q = TWOS[d]
+        return row_of(y, (xh + q) % 2, c), xl * 8 + (z + dz) % 8
 
     def r_copy(d):
-        to = along_row(d)
+        to, where = along_one(d)
         return pltpu.make_async_remote_copy(src_ref=grow.at[pl.ds(pl.multiple_of(to * 16, 16), 16)], dst_ref=grow_in.at[d],
-                                            send_sem=r_send.at[d], recv_sem=r_recv.at[d], device_id=(to, j), device_id_type=MESH)
+                                            send_sem=r_send.at[d], recv_sem=r_recv.at[d], device_id=where, device_id_type=MESH)
 
     r_copies = [r_copy(d) for d in range(15)]
     each(r_copies, "start")
@@ -303,16 +305,16 @@
 
     sums(0, 4)
 
-    total = gsum[pl.ds(pl.multiple_of(i * 16, 16), 16), :]
+    total = gsum[pl.ds(pl.multiple_of(one * 16, 16), 16), :]
     for n, copy in enumerate(r_copies):
         copy.wait_recv()
         total += grow_in[n].astype(F32)
-    gcol_in[j] = total.astype(BF16)
+    gcol_in[two] = total.astype(BF16)
 
     def c_copy(d):
-        to = along_col(d)
-        return pltpu.make_async_remote_copy(src_ref=gcol_in.at[j], dst_ref=gcol_in.at[j],
-                                            send_sem=c_send.at[d], recv_sem=c_recv.at[d], device_id=(i, to), device_id_type=MESH)
+        where = along_two(d)
+        return pltpu.make_async_remote_copy(src_ref=gcol_in.at[two], dst_ref=gcol_in.at[two],
+                                            send_sem=c_send.at[d], recv_sem=c_recv.at[d], device_id=where, device_id_type=MESH)
 
     c_copies = [c_copy(d) for d in range(15)]
     each(c_copies, "start")
@@ -321,12 +323,12 @@
     total = gcol_in[0].astype(F32)
     for d in range(1, NC):
         total += gcol_in[d].astype(F32)
-    gall[i] = (total * (1.0 / 256.0)).astype(BF16)
+    gall[one] = (total * (1.0 / 256.0)).astype(BF16)
 
     def b_copy(d):
-        to = along_row(d)
-        return pltpu.make_async_remote_copy(src_ref=gall.at[i], dst_ref=gall.at[i],
-                                            send_sem=b_send.at[d], recv_sem=b_recv.at[d], device_id=(to, j), device_id_type=MESH)
+        to, where = along_one(d)
+        return pltpu.make_async_remote_copy(src_ref=gall.at[one], dst_ref=gall.at[one],
+                                            send_sem=b_send.at[d], recv_sem=b_recv.at[d], device_id=where, device_id_type=MESH)
 
     b_copies = [b_copy(d) for d in range(15)]
     each(b_copies, "start")

time: 58.8 us -> 57.9 us (0.985)
  Pallas kernels: 56.1 us -> 55.2 us
    pallas_call x1, Pallas kernels: 56.1 us -> 55.2 us  [shards(): pl.pallas_call(kernel, out_shape=(pltpu.VMEM((1, 256, F), BF16), pltpu.VM...]
where the time goes in v4:
time: 57.9 us
  Pallas kernels  55.2 us (95%)
  local copies, waits for them, and re-layouts  1.36 us (2%)
  between operations  1.29 us (2%)
    pallas_call x1, Pallas kernels, shards(): pl.pallas_call(kernel, out_shape=(pltpu.VMEM((1, 256, F), BF16), pltpu.VM...  55.2 us
    unnamed x2, local copies, waits for them, and re-layouts  1.36 us

profile of v4, /device:TPU:1, one launch (start us, length us, event | category | flops | bytes accessed | tf_op | source)
XLA Modules:
  0.0 57.9 jit_solution(11109976805302243996)
XLA Ops:
  1.3 55.2 %shard_map.95 = (bf16[1,256,256]{2,1,0:T(8,128)(2,1)S(1)}, f32[256,256]{1,0:T(8,128)S(1)}) custom-call(bf16[256,256]{1,0:T(8,128)(2,1)} %go_hbm.1, bf16[256,256]{1,0:T(8,128)(2,1)} %pre_hbm.1, bf16[1,256,256]{2,1,0:T(8,128)(2,1)} %feat_hbm.1, bf16[256,256]{1,0:T(8,128)(2,1)} %w_hbm.1, bf16[1,1,256,128,128]{4,3,2,1,0:T(8,128)(2,1)} %tiles_ref.1, ...), custom_call_target="tpu_custom_call" | custom-call | flops 8589934592 | bytes 10485760 | tf_op jit(solution)/shard_map/pallas_call | solution.py:352
  56.5 0.7 %copy.12 = bf16[1,256,256]{2,1,0:T(8,128)(2,1)} copy(bf16[1,256,256]{2,1,0:T(8,128)(2,1)S(1)} %get-tuple-element.2) | data formatting | bytes 262144
  57.2 0.7 %copy.13 = f32[256,256]{1,0:T(8,128)} copy(f32[256,256]{1,0:T(8,128)S(1)} %get-tuple-element.3) | data formatting | bytes 524288

commit v5 on v4

--- a/solution.py
+++ b/solution.py
@@ -253,14 +253,9 @@
     spots = [p + o for p in spots for o in (0, 1 - 2 * c)]
     for d in to_core:
         d.wait_recv()
-    gt_sum = None
-    for k in range(4):
-        if k == 3:
-            late.wait_recv()
-        left = jnp.concatenate([pb[p] for p in spots[4 * k:4 * k + 4]], axis=1)
-        right = jnp.concatenate([fv[p] for p in spots[4 * k:4 * k + 4]], axis=0)
-        v = jnp.dot(left, right, preferred_element_type=F32)
-        gt_sum = v if gt_sum is None else gt_sum + v
+    late.wait_recv()
+    gt_sum = jnp.dot(jnp.concatenate([pb[p] for p in spots], axis=1), jnp.concatenate([fv[p] for p in spots], axis=0),
+                     preferred_element_type=F32)
     gsum[...] = gt_sum.T
     grow[...] = gsum[...].astype(BF16)
 

time: 57.9 us -> 57.5 us (level)
  no operation moved by 1% of the time
where the time goes in v5:
time: 57.5 us; the launch traced here: 57.4 us
  Pallas kernels  54.8 us (95%)
  local copies, waits for them, and re-layouts  1.36 us (2%)
  between operations  1.29 us (2%)
    pallas_call x1, Pallas kernels, shards(): pl.pallas_call(kernel, out_shape=(pltpu.VMEM((1, 256, F), BF16), pltpu.VM...  54.8 us
    unnamed x2, local copies, waits for them, and re-layouts  1.36 us

profile of v5, /device:TPU:1, one launch (start us, length us, event | category | flops | bytes accessed | tf_op | source)
XLA Modules:
  0.0 57.4 jit_solution(9713225626469075206)
XLA Ops:
  1.3 54.8 %shard_map.95 = (bf16[1,256,256]{2,1,0:T(8,128)(2,1)S(1)}, f32[256,256]{1,0:T(8,128)S(1)}) custom-call(bf16[256,256]{1,0:T(8,128)(2,1)} %go_hbm.1, bf16[256,256]{1,0:T(8,128)(2,1)} %pre_hbm.1, bf16[1,256,256]{2,1,0:T(8,128)(2,1)} %feat_hbm.1, bf16[256,256]{1,0:T(8,128)(2,1)} %w_hbm.1, bf16[1,1,256,128,128]{4,3,2,1,0:T(8,128)(2,1)} %tiles_ref.1, ...), custom_call_target="tpu_custom_call" | custom-call | flops 8589934592 | bytes 10485760 | tf_op jit(solution)/shard_map/pallas_call | solution.py:347
  56.1 0.7 %copy.12 = bf16[1,256,256]{2,1,0:T(8,128)(2,1)} copy(bf16[1,256,256]{2,1,0:T(8,128)(2,1)S(1)} %get-tuple-element.2) | data formatting | bytes 262144
  56.7 0.7 %copy.13 = f32[256,256]{1,0:T(8,128)} copy(f32[256,256]{1,0:T(8,128)S(1)} %get-tuple-element.3) | data formatting | bytes 524288
